TPU v7x, 32 devices: a whole 2x2x4 slice. The times are simulated.
32 devices in a mesh: groups: 2 (over x), wide: 16 (over z, y, core).
Axes of the slice: x: 2, y: 2, z: 4, core: 2. Of those that a mesh axis runs over, the one named last changes fastest.
Arguments:
- hidden_states: bfloat16 [2048, 64, 1024], P(('groups', 'wide')), parts along dimension 0, may hold values from -6 to 6
- block_owner: int32 [2048, 1], P(('groups', 'wide')), parts along dimension 0, may hold values from 0 to 15; in each aligned block of 64 rows (0 to 63, 64 to 127, ...) at most 8 rows name the same one
- token_doc: int32 [2048, 64], P(('groups', 'wide')), parts along dimension 0, may hold values from 0 to 7, never falling along the last dimension, each value on 1 to 32 neighbouring positions
- token_live: int32 [2048, 64], P(('groups', 'wide')), parts along dimension 0, may hold values 0 or 1
- proj_weight: bfloat16 [1024, 128], replicated, may hold values from -0.1875 to 0.1875
- queries: bfloat16 [2048, 128], P(('groups', 'wide')), parts along dimension 0, may hold values from -1.5 to 1.5
Outputs:
- scores: float32 [256, 1024], P(('groups', 'wide')), parts along dimension 0
There are 2 independent parts, one for each index of `groups`. A program takes and returns all parts, laid end to end along the dimension named above; an argument that names none is the same for every part. Nothing has to cross between parts.
Inputs may be any that keep to these rules, and one draw needn't show every extreme that they name: `block_owner`: among the 64 blocks of one index of wide no owner is named by more than 8 blocks, a bound that some block reaches. `token_doc`: within a block the ids never fall and every id appears.
All inputs are finite; a program needn't handle non-finite values. No bound on the sum of `token_live` on one device may be relied on, other than what follows from the above.
Results may differ from a plain program's by a relative error of at most 0.0011.
Values may be sent and summed in bfloat16 or wider, within the bound.
A program may use at most 64 MiB of HBM per device.

v0:
```python
import jax
import jax.numpy as jnp
from jax import lax
from jax.sharding import PartitionSpec as P

DOC_DEV = 8


def finish(highest):
    return jnp.where(highest > -100000000.0, highest, jnp.float32(0.0))


def slot_sources(block_owner, owner_count, capacity):
    nblocks = block_owner.shape[0]
    owners = block_owner[:, 0]
    onehot = (owners[:, None] == jnp.arange(owner_count, dtype=jnp.int32)[None, :]).astype(
        jnp.int32
    )
    earlier = jnp.cumsum(onehot, axis=0) - onehot
    rank_in = jnp.sum(earlier * onehot, axis=1)
    slot_of = owners * capacity + rank_in
    matches = slot_of[None, :] == jnp.arange(owner_count * capacity, dtype=jnp.int32)[:, None]
    picked = (
        jnp.sum(
            matches.astype(jnp.int32) * (jnp.arange(nblocks, dtype=jnp.int32)[None, :] + 1), axis=1
        )
        - 1
    )
    return jnp.where(picked < 0, nblocks, picked)


def local(hidden_states, block_owner, token_doc, token_live, proj_weight, queries):
    nblocks, block_len, model_width = hidden_states.shape
    owner_count = lax.axis_size("wide")
    capacity = max(2, (2 * nblocks + owner_count - 1) // owner_count)
    projected = jnp.dot(
        hidden_states.reshape(nblocks * block_len, model_width),
        proj_weight,
        preferred_element_type=jnp.float32,
    )
    vectors = (
        projected * lax.rsqrt(jnp.sum(projected * projected, axis=1, keepdims=True) + 1e-06)
    ).astype(jnp.bfloat16)
    doc_code = jnp.where(token_live == 1, token_doc, -1)
    source = slot_sources(block_owner, owner_count, capacity)
    query_piece = lax.all_gather(queries, "wide", axis=0, tiled=True)
    rows = query_piece.shape[0]
    similar = jnp.dot(query_piece, vectors.T, preferred_element_type=jnp.float32).reshape(
        rows, nblocks, block_len
    )
    partial_value = jnp.stack(
        [
            jnp.max(jnp.where(doc_code[None, :, :] == doc_slot, similar, -1000000000.0), axis=2)
            for doc_slot in range(DOC_DEV)
        ]
    )
    partial_value = jnp.transpose(partial_value, (2, 0, 1))
    partial_value = jnp.concatenate(
        [partial_value, jnp.full((1, DOC_DEV, rows), -1000000000.0, jnp.float32)], axis=0
    )
    slotted = jnp.take(partial_value, source, axis=0).reshape(owner_count, capacity, DOC_DEV, rows)
    gathered = jnp.max(slotted, axis=1)
    received = lax.all_to_all(gathered, "wide", split_axis=0, concat_axis=0, tiled=True)
    highest = jnp.max(received, axis=0)
    return finish(highest)


def solution(mesh):
    placed = (
        P(("groups", "wide"), None, None),
        P(("groups", "wide"), None),
        P(("groups", "wide"), None),
        P(("groups", "wide"), None),
        P(),
        P(("groups", "wide"), None),
    )
    return jax.shard_map(
        local, mesh=mesh, in_specs=placed, out_specs=P(("groups", "wide"), None), check_vma=False
    )
```

profile of v0, /device:TPU:0, one launch (start us, length us, event | category | flops | bytes accessed | tf_op | source)
XLA Modules:
  0.0 88.4 jit_solution(5283498672096399284)
XLA Ops:
  0.0 0.8 fusion.2
  0.8 0.1 reduce_window_sum.11
  0.9 0.8 select_reduce_fusion.10
  1.7 0.7 iota_add_fusion
  2.4 0.1 select_reduce_fusion.9
  2.5 0.8 broadcast_compare_fusion.6
  3.4 6.3 %multiply_reduce_fusion = (f32[4096]{0:T(1024)S(1)}, f32[4096,128]{0,1:T(8,128)S(1)}) fusion(bf16[4096,1024]{1,0:T(8,128)(2,1)} %bitcast.40, bf16[1024,128]{1,0:T(8,128)(2,1)S(1)} %copy-done), kind=kOutput, calls=%fused_computation.11 | convolution fusion | flops 1074786304 | bytes 10764288 | tf_op jit(solution)/shard_map/dot_general | solution.py:36
  9.7 23.8 %all_gather.3 = bf16[1024,128]{1,0:T(8,128)(2,1)S(1)} all-gather(bf16[64,128]{1,0:T(8,128)(2,1)S(1)} %copy-done.1), channel_id=1, replica_groups=mesh['groups'=2,'wide'=16] {'wide'}, dimensions={0}, use_global_device_ids=true | all-gather | bytes 278528 | tf_op jit(solution)/shard_map/all_gather | solution.py:46
  33.5 23.4 %select_reduce_fusion = (f32[1024,64]{0,1:T(8,128)S(1)}, f32[1024,64]{0,1:T(8,128)S(1)}, f32[1024,64]{0,1:T(8,128)S(1)}, f32[1024,64]{0,1:T(8,128)S(1)}, f32[102...) fusion(pred[64,64]{1,0:T(8,128)(4,1)S(1)} %get-tuple-element.21, ...), kind=kOutput, calls=%fused_computation.1 | convolution fusion | flops 1141374976 | bytes 4505600 | tf_op jit(solution)/shard_map/dot_general | solution.py:48
  56.9 0.2 stack.27
  57.1 0.2 stack.28
  57.3 0.2 stack.29
  57.4 0.2 stack.30
  57.6 0.2 stack.31
  57.8 0.2 stack.32
  58.0 0.2 stack.33
  58.2 0.2 stack.34
  58.4 0.1 sub.13
  58.5 4.7 %stack.35 = f32[8,1024,64]{1,0,2:T(8,128)} concatenate(f32[1,1024,64]{1,0,2:T(1,128)S(1)} %stack.27, f32[1,1024,64]{1,0,2:T(1,128)S(1)} %stack.28, f32[1,1024,64]{1,0,2:T(1,128)S(1)} %stack.29, f32[1,1024,64]{1,0,2:T(1,128)S(1)} %stack.30, f32[1,1024,64]{1,0,2:T(1,128)S(1)} %stack.31, f32[1,1024,64]{1,0,2:T(1,128)S(1)} %stack.32, f32[1,1024,64]{1,0,2:T(1,128)S(1)} %stack.33, ...), dimensions={0} | concatenate | bytes 4194304 | tf_op jit(solution)/shard_map/stack | solution.py:51
  63.2 1.7 %concatenate.3 = f32[65,8,1024]{2,1,0:T(8,128)S(1)} pad(f32[64,8,1024]{2,1,0:T(8,128)} %bitcast.41, f32[]{:T(128)} %constant.26.clone.1), padding=0_1x0_0x0_0 | pad | bytes 4227076 | tf_op jit(solution)/shard_map/concatenate | solution.py:58
  65.0 2.7 %gather_fusion = f32[128,8,1024]{2,1,0:T(8,128)} fusion(f32[65,8,1024]{2,1,0:T(8,128)S(1)} %concatenate.3, s32[1024]{0:T(1024)S(1)} %pad_clamp_fusion), kind=kCustom, calls=%fused_computation | custom fusion | bytes 8389120 | tf_op jit(solution)/shard_map/jit(_take)/gather | solution.py:61
  67.7 2.9 %select_reduce_fusion.8 = f32[16,8,1024]{2,1,0:T(8,128)S(1)} fusion(pred[16,8]{1,0:T(8,128)(4,1)S(1)} %compare_and_fusion, f32[128,8,1024]{2,1,0:T(8,128)} %gather_fusion), kind=kLoop, calls=%fused_computation.9 | loop fusion | flops 1966080 | bytes 4718720 | tf_op jit(solution)/shard_map/reduce_max | solution.py:62
  70.6 17.1 %all_to_all.5 = f32[16,8,1024]{2,1,0:T(8,128)S(1)} all-to-all(f32[16,8,1024]{2,1,0:T(8,128)S(1)} %select_reduce_fusion.8), channel_id=1, replica_groups=mesh['groups'=2,'wide'=16] {'wide'}, dimensions={0} | all-to-all | bytes 1048576 | tf_op jit(solution)/shard_map/all_to_all | solution.py:63
  87.8 0.6 compare_select_fusion
  (11 shorter events, 0.1 us)
Async XLA Ops:
  0.0 3.3 %copy-start = (bf16[1024,128]{1,0:T(8,128)(2,1)S(1)}, bf16[1024,128]{1,0:T(8,128)(2,1)}, u32[]{:S(2)}) copy-start(bf16[1024,128]{1,0:T(8,128)(2,1)} %param.10) | copy-start | bytes 786436
  3.3 6.3 %copy-start.1 = (bf16[64,128]{1,0:T(8,128)(2,1)S(1)}, bf16[64,128]{1,0:T(8,128)(2,1)}, u32[]{:S(2)}) copy-start(bf16[64,128]{1,0:T(8,128)(2,1)} %param.11) | copy-start | bytes 49156
where the time goes:
time: 88.7 us; the launch traced here: 88.4 us
  blocking collectives  40.9 us (46%)
  matrix products  29.7 us (33%)
  local copies, waits for them, and re-layouts  10.7 us (12%)
  other arithmetic  6.92 us (8%)
    all_gather x1, blocking collectives, local(): query_piece = lax.all_gather(queries, 'wide', axis=0, tiled=True)  23.8 us
    dot_general x1, matrix products, local(): jnp.dot(query_piece, vectors.T, preferred_element_type=jnp.float32)  23.4 us
    all_to_all x1, blocking collectives, local(): lax.all_to_all(gathered, 'wide', split_axis=0, concat_axis=0, tiled=True)  17.1 us
    dot_general x1, matrix products, local(): jnp.dot(hidden_states.reshape(nblocks * block_len, model_width), proj_wei...  6.28 us
    another operation x9, local copies, waits for them, and re-layouts, local(): jnp.stack([jnp.max(jnp.where(doc_code[None, :, :] == doc_slot, similar, -...  6.17 us
    reduce_max x1, other arithmetic, local(): gathered = jnp.max(slotted, axis=1)  2.93 us
    gather x1, local copies, waits for them, and re-layouts, local(): jnp.take(partial_value, source, axis=0)  2.74 us

commit v1 on v0

v1 whole, which is shorter than its diff:
```python
import functools

import jax
import jax.numpy as jnp
from jax import lax
from jax.experimental import pallas as pl
from jax.experimental.pallas import tpu as pltpu
from jax.sharding import PartitionSpec as P

DOC_DEV = 8
LOW = -1000000000.0
MESH = pl.DeviceIdType.MESH


def slot_table(owners, owner_count, capacity):
    nblocks = owners.shape[0]
    place = jnp.arange(nblocks, dtype=jnp.int32)
    same = (owners[:, None] == owners[None, :]) & (place[:, None] < place[None, :])
    rank = jnp.sum(same.astype(jnp.int32), axis=0)
    key = owners * capacity + rank
    matches = key[None, :] == jnp.arange(owner_count * capacity, dtype=jnp.int32)[:, None]
    return nblocks + jnp.sum(jnp.where(matches, place[None, :] - nblocks, 0), axis=1)


def kernel(
    n,
    capacity,
    chunk,
    piece,
    table,
    hidden,
    doc,
    live,
    weight,
    queries,
    out,
    hid,
    vec,
    codes,
    qall,
    partial,
    send,
    recv,
    hid_sem,
    qs_sem,
    qr_sem,
    s_sem,
    r_sem,
):
    nblocks, block = doc.shape
    dim = weight.shape[1]
    nq = queries.shape[0]
    tokens = nblocks * block
    pieces = tokens // piece
    chunks = (n * nq) // chunk
    me = lax.axis_index("wide")

    def stream(i):
        rows = pl.ds(pl.multiple_of(i * piece, piece), piece)
        return pltpu.make_async_copy(hidden.at[rows], hid.at[rows], hid_sem.at[i])

    @pl.loop(0, pieces)
    def _(i):
        stream(i).start()

    barrier = pltpu.get_barrier_semaphore()

    @pl.loop(1, n)
    def _(k):
        pl.semaphore_signal(
            barrier, inc=1, device_id={"wide": lax.rem(me + k, n)}, device_id_type=MESH
        )

    mine = pl.ds(pl.multiple_of(me * nq, nq), nq)

    code = jnp.where(live[...] == 1, doc[...], -1).astype(jnp.float32).astype(jnp.bfloat16)
    rows_of = lax.broadcasted_iota(jnp.int32, (nblocks, dim), 0)

    @pl.loop(0, nblocks)
    def _(b):
        pick = (rows_of == b).astype(jnp.float32).astype(jnp.bfloat16)
        codes[pl.ds(pl.multiple_of(b * block, block), block), :] = lax.dot_general(
            code, pick, (((0,), (0,)), ((), ())), preferred_element_type=jnp.float32
        )

    partial[nblocks] = jnp.full(partial.shape[1:], LOW, jnp.float32)
    qall[mine, :] = queries[...]
    pl.semaphore_wait(barrier, n - 1)

    def spread(k):
        return pltpu.make_async_remote_copy(
            src_ref=queries,
            dst_ref=qall.at[mine],
            send_sem=qs_sem.at[k],
            recv_sem=qr_sem.at[k],
            device_id={"wide": lax.rem(me + k, n)},
            device_id_type=MESH,
        )

    @pl.loop(1, n)
    def _(k):
        spread(k).start()

    @pl.loop(0, pieces)
    def _(i):
        stream(i).wait()
        rows = pl.ds(pl.multiple_of(i * piece, piece), piece)
        projected = jnp.dot(hid[rows, :], weight[...], preferred_element_type=jnp.float32)
        scale = lax.rsqrt(jnp.sum(projected * projected, axis=1, keepdims=True) + 1e-06)
        vec[rows, :] = (projected * scale).astype(jnp.bfloat16)

    @pl.loop(1, n)
    def _(k):
        spread(k).wait()

    group = 4 if nblocks % 4 == 0 else 1

    def ship(c, k):
        return pltpu.make_async_remote_copy(
            src_ref=send.at[c, k],
            dst_ref=recv.at[c, k],
            send_sem=s_sem.at[c, k],
            recv_sem=r_sem.at[c, k],
            device_id={"wide": lax.rem(me + k, n)},
            device_id_type=MESH,
        )

    @pl.loop(0, chunks)
    def _(c):
        asked = qall[pl.ds(pl.multiple_of(c * chunk, chunk), chunk), :]

        @pl.loop(0, nblocks // group)
        def _(g):
            rows = pl.ds(pl.multiple_of(g * group * block, group * block), group * block)
            similar = lax.dot_general(
                vec[rows, :], asked, (((1,), (1,)), ((), ())), preferred_element_type=jnp.float32
            )
            named = codes[rows, :]
            for b in range(group):
                part = similar[b * block : (b + 1) * block]
                which = named[b * block : (b + 1) * block]
                which = jnp.concatenate([which] * (chunk // dim), axis=1)
                for d in range(DOC_DEV):
                    kept = jnp.where(which == float(d), part, LOW)
                    partial[g * group + b, d] = jnp.max(
                        kept.reshape(block // 8, 8, chunk), axis=0
                    )

        @pl.loop(0, n)
        def _(k):
            owner = lax.rem(me + k, n)
            best = partial[table[owner * capacity]]
            for s in range(1, capacity):
                best = jnp.maximum(best, partial[table[owner * capacity + s]])
            send[c, k] = jnp.max(best, axis=1)

        @pl.loop(1, n)
        def _(k):
            ship(c, k).start()

    @pl.loop(0, chunks)
    def _(c):
        def take(k, best):
            ship(c, k).wait()
            return jnp.maximum(best, recv[c, k])

        best = lax.fori_loop(1, n, take, send[c, 0])
        out[:, pl.ds(pl.multiple_of(c * chunk, chunk), chunk)] = jnp.where(
            best > -100000000.0, best, 0.0
        )


def local(hidden_states, block_owner, token_doc, token_live, proj_weight, queries):
    nblocks, block, width = hidden_states.shape
    n = lax.axis_size("wide")
    capacity = max(2, (2 * nblocks + n - 1) // n)
    tokens = nblocks * block
    dim = proj_weight.shape[1]
    nq = queries.shape[0]
    total = n * nq
    chunk = min(256, total)
    chunks = total // chunk
    piece = min(512, tokens)
    table = slot_table(block_owner[:, 0], n, capacity)
    vmem = pl.BlockSpec(memory_space=pltpu.VMEM)
    return pl.pallas_call(
        functools.partial(kernel, n, capacity, chunk, piece),
        out_shape=jax.ShapeDtypeStruct((DOC_DEV, total), jnp.float32),
        in_specs=[
            pl.BlockSpec(memory_space=pltpu.SMEM),
            pl.BlockSpec(memory_space=pl.ANY),
            vmem,
            vmem,
            vmem,
            vmem,
        ],
        out_specs=vmem,
        scratch_shapes=[
            pltpu.VMEM((tokens, width), jnp.bfloat16),
            pltpu.VMEM((tokens, dim), jnp.bfloat16),
            pltpu.VMEM((tokens, dim), jnp.float32),
            pltpu.VMEM((total, dim), jnp.bfloat16),
            pltpu.VMEM((nblocks + 1, DOC_DEV, 8, chunk), jnp.float32),
            pltpu.VMEM((chunks, n, DOC_DEV, chunk), jnp.float32),
            pltpu.VMEM((chunks, n, DOC_DEV, chunk), jnp.float32),
            pltpu.SemaphoreType.DMA((tokens // piece,)),
            pltpu.SemaphoreType.DMA((n,)),
            pltpu.SemaphoreType.DMA((n,)),
            pltpu.SemaphoreType.DMA((chunks, n)),
            pltpu.SemaphoreType.DMA((chunks, n)),
        ],
        compiler_params=pltpu.CompilerParams(
            collective_id=0, has_side_effects=True, vmem_limit_bytes=50 * 1024 * 1024
        ),
    )(
        table,
        hidden_states.reshape(tokens, width),
        token_doc,
        token_live,
        proj_weight,
        queries,
    )


def solution(mesh):
    placed = (
        P(("groups", "wide"), None, None),
        P(("groups", "wide"), None),
        P(("groups", "wide"), None),
        P(("groups", "wide"), None),
        P(),
        P(("groups", "wide"), None),
    )
    return jax.shard_map(
        local, mesh=mesh, in_specs=placed, out_specs=P(("groups", "wide"), None), check_vma=False
    )
```

time: 88.7 us -> 59.9 us (0.68)
  Pallas kernels: 0 us -> 54.1 us
  blocking collectives: 40.9 us -> 0 us
  matrix products: 29.7 us -> 0 us
  local copies, waits for them, and re-layouts: 10.7 us -> 3.79 us
  other arithmetic: 6.92 us -> 1.59 us
    pallas_call x0 -> x1, Pallas kernels: none -> 54.1 us  [local(): pl.pallas_call(functools.partial(kernel, n, capacity, chunk, piece), out_...]
    dot_general x2 -> x0, matrix products: 29.7 us -> none  [the longest x1 23.4 us: local(): jnp.dot(query_piece, vectors.T, preferred_element_type=jnp.float32)]
    all_gather x1 -> x0, blocking collectives: 23.8 us -> none  [local(): query_piece = lax.all_gather(queries, 'wide', axis=0, tiled=True)]
    all_to_all x1 -> x0, blocking collectives: 17.1 us -> none  [local(): lax.all_to_all(gathered, 'wide', split_axis=0, concat_axis=0, tiled=True)]
    another operation x9 -> x0, local copies, waits for them, and re-layouts: 6.17 us -> none  [local(): jnp.stack([jnp.max(jnp.where(doc_code[None, :, :] == doc_slot, similar, -...]
    unnamed x4 -> x9, local copies, waits for them, and re-layouts: 0.01 us -> 3.79 us
    reduce_max x2 -> x0, other arithmetic: 2.97 us -> none  [the longest x1 2.93 us: local(): gathered = jnp.max(slotted, axis=1)]
    gather x1 -> x0, local copies, waits for them, and re-layouts: 2.74 us -> none  [local(): jnp.take(partial_value, source, axis=0)]
where the time goes in v1:
time: 59.9 us; the launch traced here: 59.5 us
  Pallas kernels  54.1 us (90%)
  local copies, waits for them, and re-layouts  3.79 us (6%)
  other arithmetic  1.59 us (3%)
    pallas_call x1, Pallas kernels, local(): pl.pallas_call(functools.partial(kernel, n, capacity, chunk, piece), out_...  54.1 us
    unnamed x9, local copies, waits for them, and re-layouts  3.79 us

profile of v1, /device:TPU:0, one launch (start us, length us, event | category | flops | bytes accessed | tf_op | source)
XLA Modules:
  0.0 59.5 jit_solution(6123228851453245537)
XLA Ops:
  0.0 0.8 %convert_reduce_fusion = s32[64]{0:T(128)S(1)} fusion(s32[64]{0:T(128)} %bitcast.4), kind=kLoop, calls=%fused_computation.2 | loop fusion | flops 20416 | bytes 512 | tf_op jit(solution)/shard_map/reduce_sum | solution.py:19
  0.8 0.7 %iota_add_fusion = (s32[64]{0:T(128)S(1)}, s32[64]{0:T(128)S(1)}) fusion(s32[64]{0:T(128)S(1)} %convert_reduce_fusion, s32[64,1]{0,1:T(1,128)} %param.7), kind=kLoop, calls=%fused_computation.5 | loop fusion | flops 192 | bytes 1024 | tf_op jit(solution)/shard_map/sub | solution.py:22
  1.5 0.1 select_reduce_fusion
  1.6 0.0 copy-start
  1.6 0.9 %copy-done = bf16[1024,128]{1,0:T(8,128)(2,1)S(1)} copy-done((bf16[1024,128]{1,0:T(8,128)(2,1)S(1)}, bf16[1024,128]{1,0:T(8,128)(2,1)}, u32[]{:S(2)}) %copy-start) | copy-done | bytes 262168
  2.5 0.0 copy-start.1
  2.5 0.8 %copy-done.1 = s32[64,64]{1,0:T(8,128)S(1)} copy-done((s32[64,64]{1,0:T(8,128)S(1)}, s32[64,64]{1,0:T(8,128)}, u32[]{:S(2)}) %copy-start.1) | copy-done | bytes 16408
  3.3 0.0 copy-start.2
  3.3 0.8 %copy-done.2 = s32[64,64]{1,0:T(8,128)S(1)} copy-done((s32[64,64]{1,0:T(8,128)S(1)}, s32[64,64]{1,0:T(8,128)}, u32[]{:S(2)}) %copy-start.2) | copy-done | bytes 16408
  4.1 0.0 copy-start.3
  4.1 0.7 %copy-done.3 = bf16[64,128]{1,0:T(8,128)(2,1)S(1)} copy-done((bf16[64,128]{1,0:T(8,128)(2,1)S(1)}, bf16[64,128]{1,0:T(8,128)(2,1)}, u32[]{:S(2)}) %copy-start.3) | copy-done | bytes 16408
  4.8 54.1 %shard_map.64 = f32[8,1024]{1,0:T(8,128)S(1)} custom-call(s32[128]{0:T(128)S(1)} %broadcast_add_fusion.table, bf16[4096,1024]{1,0:T(8,128)(2,1)} %bitcast.3, s32[64,64]{1,0:T(8,128)S(1)} %copy-done.1, s32[64,64]{1,0:T(8,128)S(1)} %copy-done.2, bf16[1024,128]{1,0:T(8,128)(2,1)S(1)} %copy-done, bf16[64,128]{1,0:T(8,128)(2,1)S(1)} %copy-done.3), custom_call_target="tpu_custom_call" | custom-call | tf_op jit(solution)/shard_map/pallas_call | solution.py:186
  58.9 0.6 %copy.8 = f32[8,1024]{1,0:T(8,128)} copy(f32[8,1024]{1,0:T(8,128)S(1)} %shard_map.64) | data formatting | bytes 65536
  (1 shorter events, 0.0 us)
Async XLA Ops:
  1.6 1.0 %copy-start = (bf16[1024,128]{1,0:T(8,128)(2,1)S(1)}, bf16[1024,128]{1,0:T(8,128)(2,1)}, u32[]{:S(2)}) copy-start(bf16[1024,128]{1,0:T(8,128)(2,1)} %weight.1) | copy-start | bytes 786436
  2.5 0.8 %copy-start.1 = (s32[64,64]{1,0:T(8,128)S(1)}, s32[64,64]{1,0:T(8,128)}, u32[]{:S(2)}) copy-start(s32[64,64]{1,0:T(8,128)} %doc.1) | copy-start | bytes 49156
  3.3 0.8 %copy-start.2 = (s32[64,64]{1,0:T(8,128)S(1)}, s32[64,64]{1,0:T(8,128)}, u32[]{:S(2)}) copy-start(s32[64,64]{1,0:T(8,128)} %live.1) | copy-start | bytes 49156
  4.1 0.7 %copy-start.3 = (bf16[64,128]{1,0:T(8,128)(2,1)S(1)}, bf16[64,128]{1,0:T(8,128)(2,1)}, u32[]{:S(2)}) copy-start(bf16[64,128]{1,0:T(8,128)(2,1)} %queries.1) | copy-start | bytes 49156

commit v2 on v1

--- a/solution.py
+++ b/solution.py
@@ -8,18 +8,25 @@
 from jax.sharding import PartitionSpec as P
 
 DOC_DEV = 8
+MOST_TOKENS = 32
 LOW = -1000000000.0
 MESH = pl.DeviceIdType.MESH
 
 
 def slot_table(owners, owner_count, capacity):
     nblocks = owners.shape[0]
-    place = jnp.arange(nblocks, dtype=jnp.int32)
-    same = (owners[:, None] == owners[None, :]) & (place[:, None] < place[None, :])
-    rank = jnp.sum(same.astype(jnp.int32), axis=0)
+    slots = owner_count * capacity
+    down = lax.broadcasted_iota(jnp.int32, (nblocks, nblocks), 0)
+    along = lax.broadcasted_iota(jnp.int32, (nblocks, nblocks), 1)
+    own = jnp.broadcast_to(owners, (nblocks, nblocks))
+    across = jnp.sum(jnp.where(down == along, own, 0), axis=0, keepdims=True)
+    earlier = jnp.where((own == across) & (along < down), 1, 0)
+    rank = jnp.sum(earlier, axis=1, keepdims=True)
     key = owners * capacity + rank
-    matches = key[None, :] == jnp.arange(owner_count * capacity, dtype=jnp.int32)[:, None]
-    return nblocks + jnp.sum(jnp.where(matches, place[None, :] - nblocks, 0), axis=1)
+    slot = lax.broadcasted_iota(jnp.int32, (nblocks, slots), 1)
+    block = lax.broadcasted_iota(jnp.int32, (nblocks, slots), 0)
+    held = jnp.where(slot == key, block - nblocks, 0)
+    return nblocks + jnp.sum(held, axis=0, keepdims=True)
 
 
 def kernel(
@@ -27,13 +34,20 @@
     capacity,
     chunk,
     piece,
-    table,
     hidden,
+    owner_hbm,
+    doc_hbm,
+    live_hbm,
+    weight_hbm,
+    queries_hbm,
+    out,
+    owners,
     doc,
     live,
     weight,
     queries,
-    out,
+    tablev,
+    table,
     hid,
     vec,
     codes,
@@ -41,6 +55,7 @@
     partial,
     send,
     recv,
+    in_sem,
     hid_sem,
     qs_sem,
     qr_sem,
@@ -59,6 +74,21 @@
         rows = pl.ds(pl.multiple_of(i * piece, piece), piece)
         return pltpu.make_async_copy(hidden.at[rows], hid.at[rows], hid_sem.at[i])
 
+    small = [
+        pltpu.make_async_copy(src, dst, in_sem.at[i])
+        for i, (src, dst) in enumerate(
+            (
+                (queries_hbm, queries),
+                (owner_hbm, owners),
+                (doc_hbm, doc),
+                (live_hbm, live),
+                (weight_hbm, weight),
+            )
+        )
+    ]
+    for copy in small:
+        copy.start()
+
     @pl.loop(0, pieces)
     def _(i):
         stream(i).start()
@@ -73,17 +103,7 @@
 
     mine = pl.ds(pl.multiple_of(me * nq, nq), nq)
 
-    code = jnp.where(live[...] == 1, doc[...], -1).astype(jnp.float32).astype(jnp.bfloat16)
-    rows_of = lax.broadcasted_iota(jnp.int32, (nblocks, dim), 0)
-
-    @pl.loop(0, nblocks)
-    def _(b):
-        pick = (rows_of == b).astype(jnp.float32).astype(jnp.bfloat16)
-        codes[pl.ds(pl.multiple_of(b * block, block), block), :] = lax.dot_general(
-            code, pick, (((0,), (0,)), ((), ())), preferred_element_type=jnp.float32
-        )
-
-    partial[nblocks] = jnp.full(partial.shape[1:], LOW, jnp.float32)
+    small[0].wait()
     qall[mine, :] = queries[...]
     pl.semaphore_wait(barrier, n - 1)
 
@@ -101,6 +121,28 @@
     def _(k):
         spread(k).start()
 
+    small[1].wait()
+    tablev[...] = slot_table(owners[...], n, capacity)
+    to_scalars = pltpu.make_async_copy(tablev, table, in_sem.at[5])
+    to_scalars.start()
+    partial[nblocks] = jnp.full(partial.shape[1:], LOW, jnp.float32)
+
+    small[2].wait()
+    small[3].wait()
+    code = jnp.where(live[...] == 1, doc[...], -1).astype(jnp.float32).astype(jnp.bfloat16)
+    unit = lax.broadcasted_iota(jnp.int32, (nblocks, dim), 0) == lax.broadcasted_iota(
+        jnp.int32, (nblocks, dim), 1
+    )
+    turned = lax.dot_general(
+        code,
+        unit.astype(jnp.float32).astype(jnp.bfloat16),
+        (((0,), (0,)), ((), ())),
+        preferred_element_type=jnp.float32,
+    )
+    for b in range(nblocks):
+        codes[b * block : (b + 1) * block, :] = jnp.broadcast_to(turned[:, b : b + 1], (block, dim))
+    small[4].wait()
+
     @pl.loop(0, pieces)
     def _(i):
         stream(i).wait()
@@ -109,11 +151,13 @@
         scale = lax.rsqrt(jnp.sum(projected * projected, axis=1, keepdims=True) + 1e-06)
         vec[rows, :] = (projected * scale).astype(jnp.bfloat16)
 
+    to_scalars.wait()
+
     @pl.loop(1, n)
     def _(k):
         spread(k).wait()
 
-    group = 4 if nblocks % 4 == 0 else 1
+    group = 8 if nblocks % 8 == 0 else 1
 
     def ship(c, k):
         return pltpu.make_async_remote_copy(
@@ -139,19 +183,23 @@
             for b in range(group):
                 part = similar[b * block : (b + 1) * block]
                 which = named[b * block : (b + 1) * block]
-                which = jnp.concatenate([which] * (chunk // dim), axis=1)
                 for d in range(DOC_DEV):
-                    kept = jnp.where(which == float(d), part, LOW)
-                    partial[g * group + b, d] = jnp.max(
-                        kept.reshape(block // 8, 8, chunk), axis=0
-                    )
+                    first = max(d, block - MOST_TOKENS * (DOC_DEV - d)) // 8 * 8
+                    last = -(-min(MOST_TOKENS * (d + 1), block - (DOC_DEV - 1 - d)) // 8) * 8
+                    keep = which[first:last] == float(d)
+                    for h in range(0, chunk, dim):
+                        kept = jnp.where(keep, part[first:last, h : h + dim], LOW)
+                        partial[g * group + b, d, :, h : h + dim] = jnp.max(
+                            kept.reshape((last - first) // 8, 8, dim), axis=0
+                        )
 
         @pl.loop(0, n)
         def _(k):
             owner = lax.rem(me + k, n)
-            best = partial[table[owner * capacity]]
-            for s in range(1, capacity):
-                best = jnp.maximum(best, partial[table[owner * capacity + s]])
+            best = None
+            for s in range(capacity):
+                at = jnp.clip(table[0, owner * capacity + s], 0, nblocks)
+                best = partial[at] if best is None else jnp.maximum(best, partial[at])
             send[c, k] = jnp.max(best, axis=1)
 
         @pl.loop(1, n)
@@ -178,24 +226,23 @@
     dim = proj_weight.shape[1]
     nq = queries.shape[0]
     total = n * nq
-    chunk = min(256, total)
+    chunk = min(512, total)
     chunks = total // chunk
     piece = min(512, tokens)
-    table = slot_table(block_owner[:, 0], n, capacity)
     vmem = pl.BlockSpec(memory_space=pltpu.VMEM)
     return pl.pallas_call(
         functools.partial(kernel, n, capacity, chunk, piece),
         out_shape=jax.ShapeDtypeStruct((DOC_DEV, total), jnp.float32),
-        in_specs=[
-            pl.BlockSpec(memory_space=pltpu.SMEM),
-            pl.BlockSpec(memory_space=pl.ANY),
-            vmem,
-            vmem,
-            vmem,
-            vmem,
-        ],
+        in_specs=[pl.BlockSpec(memory_space=pl.ANY)] * 6,
         out_specs=vmem,
         scratch_shapes=[
+            pltpu.VMEM(block_owner.shape, jnp.int32),
+            pltpu.VMEM(token_doc.shape, jnp.int32),
+            pltpu.VMEM(token_live.shape, jnp.int32),
+            pltpu.VMEM(proj_weight.shape, jnp.bfloat16),
+            pltpu.VMEM(queries.shape, jnp.bfloat16),
+            pltpu.VMEM((1, n * capacity), jnp.int32),
+            pltpu.SMEM((1, n * capacity), jnp.int32),
             pltpu.VMEM((tokens, width), jnp.bfloat16),
             pltpu.VMEM((tokens, dim), jnp.bfloat16),
             pltpu.VMEM((tokens, dim), jnp.float32),
@@ -203,6 +250,7 @@
             pltpu.VMEM((nblocks + 1, DOC_DEV, 8, chunk), jnp.float32),
             pltpu.VMEM((chunks, n, DOC_DEV, chunk), jnp.float32),
             pltpu.VMEM((chunks, n, DOC_DEV, chunk), jnp.float32),
+            pltpu.SemaphoreType.DMA((6,)),
             pltpu.SemaphoreType.DMA((tokens // piece,)),
             pltpu.SemaphoreType.DMA((n,)),
             pltpu.SemaphoreType.DMA((n,)),
@@ -213,8 +261,8 @@
             collective_id=0, has_side_effects=True, vmem_limit_bytes=50 * 1024 * 1024
         ),
     )(
-        table,
         hidden_states.reshape(tokens, width),
+        block_owner,
         token_doc,
         token_live,
         proj_weight,

time: 59.9 us -> 41.6 us (0.69)
  Pallas kernels: 54.1 us -> 36.7 us
  other arithmetic: 1.59 us -> 0 us
  local copies, waits for them, and re-layouts: 3.79 us -> 4.54 us
    pallas_call x1, Pallas kernels: 54.1 us -> 36.7 us  [local(): pl.pallas_call(functools.partial(kernel, n, capacity, chunk, piece), out_...]
    reduce_sum x2 -> x0, other arithmetic: 0.92 us -> none  [the longest x1 0.82 us: slot_table(): rank = jnp.sum(same.astype(jnp.int32), axis=0)]
    unnamed x9 -> x10, local copies, waits for them, and re-layouts: 3.79 us -> 4.54 us
    sub x1 -> x0, other arithmetic: 0.66 us -> none  [slot_table(): place[None, :] - nblocks]
where the time goes in v2:
time: 41.6 us; the launch traced here: 41.2 us
  Pallas kernels  36.7 us (88%)
  local copies, waits for them, and re-layouts  4.54 us (11%)
    pallas_call x1, Pallas kernels, local(): pl.pallas_call(functools.partial(kernel, n, capacity, chunk, piece), out_...  36.7 us
    unnamed x10, local copies, waits for them, and re-layouts  4.54 us

profile of v2, /device:TPU:0, one launch (start us, length us, event | category | flops | bytes accessed | tf_op | source)
XLA Modules:
  0.0 41.2 jit_solution(14590563230941061586)
XLA Ops:
  0.0 0.7 %copy.7.owner_hbm = s32[64,1]{1,0:T(8,128)S(1)} copy(s32[64,1]{0,1:T(1,128)} %param.7) | data formatting | bytes 512 | tf_op args[1]
  0.7 0.0 copy-start
  0.7 0.9 %copy-done = bf16[1024,128]{1,0:T(8,128)(2,1)S(1)} copy-done((bf16[1024,128]{1,0:T(8,128)(2,1)S(1)}, bf16[1024,128]{1,0:T(8,128)(2,1)}, u32[]{:S(2)}) %copy-start) | copy-done | bytes 262168
  1.7 0.0 copy-start.1
  1.7 0.8 %copy-done.1 = s32[64,64]{1,0:T(8,128)S(1)} copy-done((s32[64,64]{1,0:T(8,128)S(1)}, s32[64,64]{1,0:T(8,128)}, u32[]{:S(2)}) %copy-start.1) | copy-done | bytes 16408
  2.5 0.0 copy-start.2
  2.5 0.8 %copy-done.2 = s32[64,64]{1,0:T(8,128)S(1)} copy-done((s32[64,64]{1,0:T(8,128)S(1)}, s32[64,64]{1,0:T(8,128)}, u32[]{:S(2)}) %copy-start.2) | copy-done | bytes 16408
  3.2 0.0 copy-start.3
  3.2 0.7 %copy-done.3 = bf16[64,128]{1,0:T(8,128)(2,1)S(1)} copy-done((bf16[64,128]{1,0:T(8,128)(2,1)S(1)}, bf16[64,128]{1,0:T(8,128)(2,1)}, u32[]{:S(2)}) %copy-start.3) | copy-done | bytes 16408
  3.9 36.7 %shard_map.64 = f32[8,1024]{1,0:T(8,128)S(1)} custom-call(bf16[4096,1024]{1,0:T(8,128)(2,1)} %bitcast.1, s32[64,1]{1,0:T(8,128)S(1)} %copy.7.owner_hbm, s32[64,64]{1,0:T(8,128)S(1)} %copy-done.1, s32[64,64]{1,0:T(8,128)S(1)} %copy-done.2, bf16[1024,128]{1,0:T(8,128)(2,1)S(1)} %copy-done, bf16[64,128]{1,0:T(8,128)(2,1)S(1)} %copy-done.3), custom_call_target="tpu_custom_call" | custom-call | tf_op jit(solution)/shard_map/pallas_call | solution.py:233
  40.6 0.6 %copy.9 = f32[8,1024]{1,0:T(8,128)} copy(f32[8,1024]{1,0:T(8,128)S(1)} %shard_map.64) | data formatting | bytes 65536
Async XLA Ops:
  0.7 0.9 %copy-start = (bf16[1024,128]{1,0:T(8,128)(2,1)S(1)}, bf16[1024,128]{1,0:T(8,128)(2,1)}, u32[]{:S(2)}) copy-start(bf16[1024,128]{1,0:T(8,128)(2,1)} %weight_hbm.1) | copy-start | bytes 786436
  1.7 0.8 %copy-start.1 = (s32[64,64]{1,0:T(8,128)S(1)}, s32[64,64]{1,0:T(8,128)}, u32[]{:S(2)}) copy-start(s32[64,64]{1,0:T(8,128)} %doc_hbm.1) | copy-start | bytes 49156
  2.5 0.8 %copy-start.2 = (s32[64,64]{1,0:T(8,128)S(1)}, s32[64,64]{1,0:T(8,128)}, u32[]{:S(2)}) copy-start(s32[64,64]{1,0:T(8,128)} %live_hbm.1) | copy-start | bytes 49156
  3.2 0.7 %copy-start.3 = (bf16[64,128]{1,0:T(8,128)(2,1)S(1)}, bf16[64,128]{1,0:T(8,128)(2,1)}, u32[]{:S(2)}) copy-start(bf16[64,128]{1,0:T(8,128)(2,1)} %queries_hbm.1) | copy-start | bytes 49156

commit v3 on v2

--- a/solution.py
+++ b/solution.py
@@ -157,7 +157,7 @@
     def _(k):
         spread(k).wait()
 
-    group = 8 if nblocks % 8 == 0 else 1
+    group = 16 if nblocks % 16 == 0 else 1
 
     def ship(c, k):
         return pltpu.make_async_remote_copy(
@@ -202,9 +202,9 @@
                 best = partial[at] if best is None else jnp.maximum(best, partial[at])
             send[c, k] = jnp.max(best, axis=1)
 
-        @pl.loop(1, n)
-        def _(k):
-            ship(c, k).start()
+            @pl.when(k > 0)
+            def _():
+                ship(c, k).start()
 
     @pl.loop(0, chunks)
     def _(c):

time: 41.6 us -> 39 us (0.938)
  Pallas kernels: 36.7 us -> 34 us
    pallas_call x1, Pallas kernels: 36.7 us -> 34 us  [local(): pl.pallas_call(functools.partial(kernel, n, capacity, chunk, piece), out_...]
where the time goes in v3:
time: 39 us; the launch traced here: 38.6 us
  Pallas kernels  34 us (87%)
  local copies, waits for them, and re-layouts  4.54 us (12%)
    pallas_call x1, Pallas kernels, local(): pl.pallas_call(functools.partial(kernel, n, capacity, chunk, piece), out_...  34 us
    unnamed x10, local copies, waits for them, and re-layouts  4.54 us

profile of v3, /device:TPU:0, one launch (start us, length us, event | category | flops | bytes accessed | tf_op | source)
XLA Modules:
  0.0 38.6 jit_solution(17502185639466743404)
XLA Ops:
  0.0 0.7 %copy.7.owner_hbm = s32[64,1]{1,0:T(8,128)S(1)} copy(s32[64,1]{0,1:T(1,128)} %param.7) | data formatting | bytes 512 | tf_op args[1]
  0.7 0.0 copy-start
  0.7 0.9 %copy-done = bf16[1024,128]{1,0:T(8,128)(2,1)S(1)} copy-done((bf16[1024,128]{1,0:T(8,128)(2,1)S(1)}, bf16[1024,128]{1,0:T(8,128)(2,1)}, u32[]{:S(2)}) %copy-start) | copy-done | bytes 262168
  1.7 0.0 copy-start.1
  1.7 0.8 %copy-done.1 = s32[64,64]{1,0:T(8,128)S(1)} copy-done((s32[64,64]{1,0:T(8,128)S(1)}, s32[64,64]{1,0:T(8,128)}, u32[]{:S(2)}) %copy-start.1) | copy-done | bytes 16408
  2.5 0.0 copy-start.2
  2.5 0.8 %copy-done.2 = s32[64,64]{1,0:T(8,128)S(1)} copy-done((s32[64,64]{1,0:T(8,128)S(1)}, s32[64,64]{1,0:T(8,128)}, u32[]{:S(2)}) %copy-start.2) | copy-done | bytes 16408
  3.2 0.0 copy-start.3
  3.2 0.7 %copy-done.3 = bf16[64,128]{1,0:T(8,128)(2,1)S(1)} copy-done((bf16[64,128]{1,0:T(8,128)(2,1)S(1)}, bf16[64,128]{1,0:T(8,128)(2,1)}, u32[]{:S(2)}) %copy-start.3) | copy-done | bytes 16408
  3.9 34.0 %shard_map.64 = f32[8,1024]{1,0:T(8,128)S(1)} custom-call(bf16[4096,1024]{1,0:T(8,128)(2,1)} %bitcast.1, s32[64,1]{1,0:T(8,128)S(1)} %copy.7.owner_hbm, s32[64,64]{1,0:T(8,128)S(1)} %copy-done.1, s32[64,64]{1,0:T(8,128)S(1)} %copy-done.2, bf16[1024,128]{1,0:T(8,128)(2,1)S(1)} %copy-done, bf16[64,128]{1,0:T(8,128)(2,1)S(1)} %copy-done.3), custom_call_target="tpu_custom_call" | custom-call | tf_op jit(solution)/shard_map/pallas_call | solution.py:233
  37.9 0.6 %copy.9 = f32[8,1024]{1,0:T(8,128)} copy(f32[8,1024]{1,0:T(8,128)S(1)} %shard_map.64) | data formatting | bytes 65536
Async XLA Ops:
  0.7 0.9 %copy-start = (bf16[1024,128]{1,0:T(8,128)(2,1)S(1)}, bf16[1024,128]{1,0:T(8,128)(2,1)}, u32[]{:S(2)}) copy-start(bf16[1024,128]{1,0:T(8,128)(2,1)} %weight_hbm.1) | copy-start | bytes 786436
  1.7 0.8 %copy-start.1 = (s32[64,64]{1,0:T(8,128)S(1)}, s32[64,64]{1,0:T(8,128)}, u32[]{:S(2)}) copy-start(s32[64,64]{1,0:T(8,128)} %doc_hbm.1) | copy-start | bytes 49156
  2.5 0.8 %copy-start.2 = (s32[64,64]{1,0:T(8,128)S(1)}, s32[64,64]{1,0:T(8,128)}, u32[]{:S(2)}) copy-start(s32[64,64]{1,0:T(8,128)} %live_hbm.1) | copy-start | bytes 49156
  3.2 0.7 %copy-start.3 = (bf16[64,128]{1,0:T(8,128)(2,1)S(1)}, bf16[64,128]{1,0:T(8,128)(2,1)}, u32[]{:S(2)}) copy-start(bf16[64,128]{1,0:T(8,128)(2,1)} %queries_hbm.1) | copy-start | bytes 49156

commit v4 on v3

--- a/solution.py
+++ b/solution.py
@@ -157,7 +157,7 @@
     def _(k):
         spread(k).wait()
 
-    group = 16 if nblocks % 16 == 0 else 1
+    group = 32 if nblocks % 32 == 0 else 1
 
     def ship(c, k):
         return pltpu.make_async_remote_copy(

time: 39 us -> 38.6 us (0.990)
  Pallas kernels: 34 us -> 33.6 us
where the time goes in v4:
time: 38.6 us; the launch traced here: 38.2 us
  Pallas kernels  33.6 us (87%)
  local copies, waits for them, and re-layouts  4.54 us (12%)
    pallas_call x1, Pallas kernels, local(): pl.pallas_call(functools.partial(kernel, n, capacity, chunk, piece), out_...  33.6 us
    unnamed x10, local copies, waits for them, and re-layouts  4.54 us

profile of v4, /device:TPU:0, one launch (start us, length us, event | category | flops | bytes accessed | tf_op | source)
XLA Modules:
  0.0 38.2 jit_solution(2788545284201130307)
XLA Ops:
  0.0 0.7 %copy.7.owner_hbm = s32[64,1]{1,0:T(8,128)S(1)} copy(s32[64,1]{0,1:T(1,128)} %param.7) | data formatting | bytes 512 | tf_op args[1]
  0.7 0.0 copy-start
  0.7 0.9 %copy-done = bf16[1024,128]{1,0:T(8,128)(2,1)S(1)} copy-done((bf16[1024,128]{1,0:T(8,128)(2,1)S(1)}, bf16[1024,128]{1,0:T(8,128)(2,1)}, u32[]{:S(2)}) %copy-start) | copy-done | bytes 262168
  1.7 0.0 copy-start.1
  1.7 0.8 %copy-done.1 = s32[64,64]{1,0:T(8,128)S(1)} copy-done((s32[64,64]{1,0:T(8,128)S(1)}, s32[64,64]{1,0:T(8,128)}, u32[]{:S(2)}) %copy-start.1) | copy-done | bytes 16408
  2.5 0.0 copy-start.2
  2.5 0.8 %copy-done.2 = s32[64,64]{1,0:T(8,128)S(1)} copy-done((s32[64,64]{1,0:T(8,128)S(1)}, s32[64,64]{1,0:T(8,128)}, u32[]{:S(2)}) %copy-start.2) | copy-done | bytes 16408
  3.2 0.0 copy-start.3
  3.2 0.7 %copy-done.3 = bf16[64,128]{1,0:T(8,128)(2,1)S(1)} copy-done((bf16[64,128]{1,0:T(8,128)(2,1)S(1)}, bf16[64,128]{1,0:T(8,128)(2,1)}, u32[]{:S(2)}) %copy-start.3) | copy-done | bytes 16408
  3.9 33.6 %shard_map.64 = f32[8,1024]{1,0:T(8,128)S(1)} custom-call(bf16[4096,1024]{1,0:T(8,128)(2,1)} %bitcast.1, s32[64,1]{1,0:T(8,128)S(1)} %copy.7.owner_hbm, s32[64,64]{1,0:T(8,128)S(1)} %copy-done.1, s32[64,64]{1,0:T(8,128)S(1)} %copy-done.2, bf16[1024,128]{1,0:T(8,128)(2,1)S(1)} %copy-done, bf16[64,128]{1,0:T(8,128)(2,1)S(1)} %copy-done.3), custom_call_target="tpu_custom_call" | custom-call | tf_op jit(solution)/shard_map/pallas_call | solution.py:233
  37.6 0.6 %copy.9 = f32[8,1024]{1,0:T(8,128)} copy(f32[8,1024]{1,0:T(8,128)S(1)} %shard_map.64) | data formatting | bytes 65536
Async XLA Ops:
  0.7 0.9 %copy-start = (bf16[1024,128]{1,0:T(8,128)(2,1)S(1)}, bf16[1024,128]{1,0:T(8,128)(2,1)}, u32[]{:S(2)}) copy-start(bf16[1024,128]{1,0:T(8,128)(2,1)} %weight_hbm.1) | copy-start | bytes 786436
  1.7 0.8 %copy-start.1 = (s32[64,64]{1,0:T(8,128)S(1)}, s32[64,64]{1,0:T(8,128)}, u32[]{:S(2)}) copy-start(s32[64,64]{1,0:T(8,128)} %doc_hbm.1) | copy-start | bytes 49156
  2.5 0.8 %copy-start.2 = (s32[64,64]{1,0:T(8,128)S(1)}, s32[64,64]{1,0:T(8,128)}, u32[]{:S(2)}) copy-start(s32[64,64]{1,0:T(8,128)} %live_hbm.1) | copy-start | bytes 49156
  3.2 0.7 %copy-start.3 = (bf16[64,128]{1,0:T(8,128)(2,1)S(1)}, bf16[64,128]{1,0:T(8,128)(2,1)}, u32[]{:S(2)}) copy-start(bf16[64,128]{1,0:T(8,128)(2,1)} %queries_hbm.1) | copy-start | bytes 49156
